TPU v7x, 32 devices: a whole 2x2x4 slice. The times are simulated.
32 devices in a mesh: dp: 2 (over x), seq: 2 (over core), expert: 8 (over z, y).
Axes of the slice: x: 2, y: 2, z: 4, core: 2. Of those that a mesh axis runs over, the one named last changes fastest.
Arguments:
- out_grad: bfloat16 [4096, 2048], P(('dp', 'seq', 'expert')), may hold values from -6 to 6
- saved_act: bfloat16 [4096, 8, 768], P(('dp', 'seq', 'expert')), may hold values from -0.29882812 to 0.29882812
- gate_probs: float32 [4096, 8], P(('dp', 'seq', 'expert')), may hold values from 0.02 to 0.6
- routes: int32 [4096, 8], P(('dp', 'seq', 'expert')), may hold values from 0 to 15, all different within a row; in each aligned block of 128 rows (0 to 127, 128 to 255, ...) at most 72 rows name the same one
- w_down: bfloat16 [16, 768, 2048], P(('seq', 'expert'), 'dp'), may hold values from -0.21875 to 0.21875
Outputs:
- act_grad: bfloat16 [4096, 8, 768], P(('dp', 'seq', 'expert'))
- prob_grad: float32 [4096, 8], P(('dp', 'seq', 'expert'))
- weight_grad: bfloat16 [16, 768, 2048], P(('seq', 'expert'), 'dp')
Inputs may be any that keep to these rules, and one draw needn't show every extreme that they name: `routes`: within the rows of one device (aligned blocks of 128 tokens) no expert is named by more than 72 tokens, a bound that some block reaches; each token names 8 different experts.
All inputs are finite; a program needn't handle non-finite values.
Results may differ from a plain program's by a relative error of at most 0.014.
Values may be sent and summed in bfloat16 or wider, within the bound.
A program may use at most 128 MiB of HBM per device.

v0:
```python
import jax
import jax.numpy as jnp
from jax import lax
from jax.sharding import PartitionSpec as P


def local(out_grad, saved_act, gate_probs, routes, w_down):
    token_count = routes.shape[0]
    top_count = routes.shape[1]
    hidden_width = saved_act.shape[2]
    feature_width = out_grad.shape[1]
    owners = lax.axis_size(("seq", "expert"))
    pair_count = token_count * top_count
    most_rows = max(2, min(token_count, pair_count // owners + pair_count // (8 * owners)))
    capacity = owners * most_rows
    expert_of = routes.reshape(pair_count)
    one_hot = (expert_of[:, None] == jnp.arange(owners, dtype=jnp.int32)[None, :]).astype(jnp.int32)
    rank_of = jnp.sum((jnp.cumsum(one_hot, axis=0) - one_hot) * one_hot, axis=1)
    slot_of = expert_of * most_rows + rank_of
    source_row = (
        jnp.zeros((capacity,), jnp.int32).at[slot_of].set(jnp.arange(pair_count, dtype=jnp.int32))
    )
    prob_rows = jnp.zeros((capacity,), jnp.float32).at[slot_of].set(gate_probs.reshape(pair_count))
    grad_rows = jnp.take(out_grad, source_row // top_count, axis=0)
    act_rows = jnp.take(saved_act.reshape(pair_count, hidden_width), source_row, axis=0)
    send_grad = grad_rows.reshape(owners, most_rows * feature_width)
    send_act = act_rows.reshape(owners, most_rows * hidden_width)
    send_prob = prob_rows.reshape(owners, most_rows)
    arrived = (
        lax.all_to_all(send_grad, ("seq", "expert"), split_axis=0, concat_axis=0, tiled=True),
        lax.all_to_all(send_act, ("seq", "expert"), split_axis=0, concat_axis=0, tiled=True),
        lax.all_to_all(
            send_prob.astype(jnp.bfloat16),
            ("seq", "expert"),
            split_axis=0,
            concat_axis=0,
            tiled=True,
        ).astype(send_prob.dtype),
    )
    recv_grad = arrived[0].reshape(capacity, feature_width)
    recv_act = arrived[1].reshape(capacity, hidden_width)
    recv_prob = arrived[2].reshape(capacity)
    expert_grad = lax.dot_general(
        recv_grad,
        lax.all_gather(w_down, "dp", axis=1, tiled=True)[0],
        (((1,), (1,)), ((), ())),
        preferred_element_type=jnp.float32,
    )
    act_back = (recv_prob[:, None] * expert_grad).astype(jnp.bfloat16)
    prob_back = jnp.sum(recv_act.astype(jnp.float32) * expert_grad, axis=1)
    scaled = (recv_prob[:, None] * recv_grad.astype(jnp.float32)).astype(jnp.bfloat16)
    weight_part = lax.psum_scatter(
        lax.dot_general(
            recv_act, scaled, (((0,), (0,)), ((), ())), preferred_element_type=jnp.float32
        ).astype(jnp.bfloat16),
        "dp",
        scatter_dimension=0,
        tiled=True,
    )
    weight_grad = weight_part.reshape(w_down.shape)
    back_act = act_back.reshape(owners, most_rows * hidden_width)
    back_prob = prob_back.reshape(owners, most_rows)
    returned = (
        lax.all_to_all(back_act, ("seq", "expert"), split_axis=0, concat_axis=0, tiled=True),
        lax.all_to_all(
            back_prob.astype(jnp.bfloat16),
            ("seq", "expert"),
            split_axis=0,
            concat_axis=0,
            tiled=True,
        ).astype(back_prob.dtype),
    )
    slot_grad = returned[0].reshape(capacity, hidden_width)
    slot_prob = returned[1].reshape(capacity)
    act_grad = jnp.take(slot_grad, slot_of, axis=0).reshape(token_count, top_count, hidden_width)
    prob_grad = jnp.take(slot_prob, slot_of, axis=0).reshape(token_count, top_count)
    return (act_grad, prob_grad, weight_grad)


def solution(mesh):
    in_specs = (
        P(("dp", "seq", "expert"), None),
        P(("dp", "seq", "expert"), None, None),
        P(("dp", "seq", "expert"), None),
        P(("dp", "seq", "expert"), None),
        P(("seq", "expert"), "dp", None),
    )
    out_specs = (
        P(("dp", "seq", "expert"), None, None),
        P(("dp", "seq", "expert"), None),
        P(("seq", "expert"), "dp", None),
    )
    return jax.shard_map(local, mesh=mesh, in_specs=in_specs, out_specs=out_specs, check_vma=False)
```

profile of v0, /device:TPU:0, one launch (start us, length us, event | category | flops | bytes accessed | tf_op | source)
XLA Modules:
  0.0 490.4 jit_solution(15474529246030302256)
XLA Ops:
  19.3 7.4 %all-to-all-start = ((bf16[16,1,72]{2,1,0:T(2,128)(2,1)}), bf16[16,1,72]{2,1,0:T(2,128)(2,1)S(1)}, u32[]{:S(2)}, u32[]{:S(2)}) async-start(bf16[16,1,72]{2,1,0:T(2,128)(2,1)} %convert_element_type.104), calls=%async_computation | async-start | bytes 16384 | tf_op jit(solution)/shard_map/all_to_all | solution.py:32
  41.3 6.0 %gather_fusion = bf16[1152,2048]{1,0:T(8,128)(2,1)} fusion(bf16[128,2048]{1,0:T(8,128)(2,1)S(1)} %copy-done.2, s32[2048]{0:T(1024)S(1)} %pad_clamp_fusion.1), kind=kCustom, calls=%fused_computation | custom fusion | bytes 9441792 | tf_op jit(solution)/shard_map/jit(_take)/gather | solution.py:24
  66.3 6.2 %all-to-all-start.3 = ((bf16[16,2,27648]{2,1,0:T(2,128)(2,1)}), bf16[16,2,27648]{2,1,0:T(2,128)(2,1)S(1)}, u32[]{:S(2)}, u32[]{:S(2)}) async-start(bf16[16,2,27648]{2,1,0:T(2,128)(2,1)} %reshape.299), calls=%async_computation.3 | async-start | bytes 3538944 | tf_op jit(solution)/shard_map/all_to_all | solution.py:31
  77.3 6.8 %reduce.15 = bf16[16,147456]{1,0:T(8,128)(2,1)} reduce(bf16[16,1,147456]{2,0,1:T(8,128)(2,1)} %broadcast_select_fusion, bf16[]{:T(256)} %broadcast.127), dimensions={1}, to_apply=%copy.40.reduce_sub_computation | reduce | bytes 9437186 | tf_op jit(solution)/shard_map/jit(_take)/select_n | solution.py:24
  84.1 7.3 %reshape.295 = bf16[16,2,73728]{2,1,0:T(2,128)(2,1)} reshape(bf16[16,147456]{1,0:T(8,128)(2,1)} %reduce.15) | data formatting | bytes 9437184
  91.4 22.0 %all-to-all-done.3 = bf16[16,2,27648]{2,1,0:T(2,128)(2,1)S(1)} async-done(((bf16[16,2,27648]{2,1,0:T(2,128)(2,1)}), bf16[16,2,27648]{2,1,0:T(2,128)(2,1)S(1)}, u32[]{:S(2)}, u32[]{:S(2)}) %all-to-all-start.3) | async-done | bytes 1769504 | tf_op jit(solution)/shard_map/all_to_all | solution.py:31
  123.2 17.7 %mul.57 = f32[16,1,147456]{2,1,0:T(1,128)} reshape(f32[16,72,2048]{2,1,0:T(8,128)} %mul.56) | data formatting | bytes 18874368 | tf_op jit(solution)/shard_map/mul | solution.py:51
  140.9 6.3 %reshape.300 = bf16[16,1,55296]{2,1,0:T(2,128)(2,1)} reshape(bf16[16,2,27648]{2,1,0:T(2,128)(2,1)S(1)} %all-to-all-done.3) | data formatting | bytes 3538944
  147.2 39.0 %reduce.3 = bf16[16,55296]{1,0:T(8,128)(2,1)} reduce(bf16[16,1,55296]{2,1,0:T(2,128)(2,1)} %reshape.300, bf16[]{:T(256)} %constant.87), dimensions={1}, to_apply=%all_to_all.26.reduce_sub_computation | reduce | bytes 3538946 | tf_op jit(solution)/shard_map/all_to_all | solution.py:31
  188.3 30.1 %all-to-all-done.1 = bf16[16,2,73728]{2,1,0:T(2,128)(2,1)} async-done(((bf16[16,2,73728]{2,1,0:T(2,128)(2,1)}), bf16[16,2,73728]{2,1,0:T(2,128)(2,1)}, u32[]{:S(2)}, u32[]{:S(2)}) %all-to-all-start.1) | async-done | bytes 4718624 | tf_op jit(solution)/shard_map/all_to_all | solution.py:30
  218.4 12.8 %reshape.296 = bf16[16,1,147456]{2,1,0:T(2,128)(2,1)} reshape(bf16[16,2,73728]{2,1,0:T(2,128)(2,1)} %all-to-all-done.1) | data formatting | bytes 9437184
  231.3 62.7 %convert_reduce_fusion = (bf16[16,147456]{1,0:T(8,128)(2,1)}, bf16[16,147456]{1,0:T(8,128)(2,1)}) fusion(f32[16,1,147456]{2,1,0:T(1,128)} %mul.57, bf16[16,1,147456]{2,1,0:T(2,128)(2,1)} %reshape.296), kind=kLoop, calls=%fused_computation.6 | loop fusion | flops 7077888 | bytes 23592960 | tf_op jit(solution)/shard_map/convert_element_type | solution.py:51
  294.0 5.4 %convert_element_type.99 = bf16[1152,2048]{1,0:T(8,128)(2,1)} reshape(bf16[16,147456]{1,0:T(8,128)(2,1)} %get-tuple-element.12) | data formatting | bytes 9437184 | tf_op jit(solution)/shard_map/convert_element_type | solution.py:51
  299.4 8.1 %convolution_convert_fusion = bf16[768,2048]{1,0:T(8,128)(2,1)} fusion(bf16[1152,768]{1,0:T(8,128)(2,1)S(1)} %reshape.220, bf16[1152,2048]{1,0:T(8,128)(2,1)} %convert_element_type.99), kind=kOutput, calls=%fused_computation.9 | convolution fusion | flops 3625451520 | bytes 9633792 | tf_op jit(solution)/shard_map/dot_general | solution.py:53
  309.8 5.3 %reshape.217 = bf16[1152,2048]{1,0:T(8,128)(2,1)} reshape(bf16[16,147456]{1,0:T(8,128)(2,1)} %get-tuple-element.13) | data formatting | bytes 9437184 | tf_op jit(solution)/shard_map/reshape | solution.py:40
  315.1 9.8 %multiply_reduce_fusion = (bf16[1152]{0:T(1024)(128)(2,1)S(1)}, bf16[1152,768]{0,1:T(8,128)(2,1)}) fusion(bf16[1152,768]{0,1:T(8,128)(2,1)S(1)} %copy-done.4, f32[1152]{0:T(1024)S(1)} %reshape.222, bf16[1152,2048]{1,0:T(8,128)(2,1)} %reshape.217, bf16[1,768,2048]{2,1,0:T(8,128)(2,1)} %all-gather.2.cloned.1.call-done), kind=kOutput, calls=%fused_computation.7 | convolution fusion | flops 3628301312 | bytes 11410176 | tf_op jit(solution)/shard_map/dot_general | solution.py:43
  325.6 8.1 %all-to-all-start.4 = ((bf16[16,1,72]{2,1,0:T(2,128)(2,1)}), bf16[16,1,72]{2,1,0:T(2,128)(2,1)S(1)}, u32[]{:S(2)}, u32[]{:S(2)}) async-start(bf16[16,1,72]{2,1,0:T(2,128)(2,1)} %convert_element_type.105), calls=%async_computation.4 | async-start | bytes 16384 | tf_op jit(solution)/shard_map/all_to_all | solution.py:65
  340.0 38.5 %reduce.16 = bf16[16,55296]{1,0:T(8,128)(2,1)S(1)} reduce(bf16[16,1,55296]{2,1,0:T(2,128)(2,1)} %all_to_all.28, bf16[]{:T(256)} %broadcast.127), dimensions={1}, to_apply=%all_to_all.28.reduce_sub_computation | reduce | bytes 3538946 | tf_op jit(solution)/shard_map/all_to_all | solution.py:64
  380.8 6.3 %all-to-all-start.2 = ((bf16[16,2,27648]{2,1,0:T(2,128)(2,1)}), bf16[16,2,27648]{2,1,0:T(2,128)(2,1)S(1)}, u32[]{:S(2)}, u32[]{:S(2)}) async-start(bf16[16,2,27648]{2,1,0:T(2,128)(2,1)} %reshape.297), calls=%async_computation.2 | async-start | bytes 3538944 | tf_op jit(solution)/shard_map/all_to_all | solution.py:64
  387.3 6.2 %gather_fusion.3 = f32[1024]{0:T(1024)S(1)} fusion(f32[1152]{0:T(1024)S(1)} %reshape.223, s32[1024]{0:T(1024)S(1)} %broadcast_clamp_fusion), kind=kCustom, calls=%fused_computation.3 | custom fusion | bytes 12288 | tf_op jit(solution)/shard_map/jit(_take)/gather | solution.py:76
  394.3 33.8 %all-to-all-done.2 = bf16[16,2,27648]{2,1,0:T(2,128)(2,1)S(1)} async-done(((bf16[16,2,27648]{2,1,0:T(2,128)(2,1)}), bf16[16,2,27648]{2,1,0:T(2,128)(2,1)S(1)}, u32[]{:S(2)}, u32[]{:S(2)}) %all-to-all-start.2) | async-done | bytes 1769504 | tf_op jit(solution)/shard_map/all_to_all | solution.py:64
  428.1 6.2 %reshape.298 = bf16[16,1,55296]{2,1,0:T(2,128)(2,1)} reshape(bf16[16,2,27648]{2,1,0:T(2,128)(2,1)S(1)} %all-to-all-done.2) | data formatting | bytes 3538944
  434.3 39.0 %reduce.2 = bf16[16,55296]{1,0:T(8,128)(2,1)} reduce(bf16[16,1,55296]{2,1,0:T(2,128)(2,1)} %reshape.298, bf16[]{:T(256)} %constant.87), dimensions={1}, to_apply=%all_to_all.25.reduce_sub_computation | reduce | bytes 3538946 | tf_op jit(solution)/shard_map/all_to_all | solution.py:64
  475.4 5.2 %gather_fusion.1 = bf16[1024,768]{1,0:T(8,128)(2,1)} fusion(bf16[1152,768]{1,0:T(8,128)(2,1)S(1)} %reshape.218, s32[1024]{0:T(1024)S(1)} %broadcast_clamp_fusion), kind=kCustom, calls=%fused_computation.1 | custom fusion | bytes 3149824 | tf_op jit(solution)/shard_map/jit(_take)/gather | solution.py:75
  (78 shorter events, 79.5 us)
Async XLA Ops:
  7.2 26.0 %copy-start = (bf16[128,8,768]{2,1,0:T(8,128)(2,1)S(1)}, bf16[128,8,768]{2,1,0:T(8,128)(2,1)}, u32[]{:S(2)}) copy-start(bf16[128,8,768]{2,1,0:T(8,128)(2,1)} %param.6) | copy-start | bytes 4718596
  19.3 47.0 %all-to-all-start = ((bf16[16,1,72]{2,1,0:T(2,128)(2,1)}), bf16[16,1,72]{2,1,0:T(2,128)(2,1)S(1)}, u32[]{:S(2)}, u32[]{:S(2)}) async-start(bf16[16,1,72]{2,1,0:T(2,128)(2,1)} %convert_element_type.104), calls=%async_computation | async-start | bytes 16384 | tf_op jit(solution)/shard_map/all_to_all | solution.py:32
  37.8 1.8 copy-start.3
  37.8 3.5 copy-start.2
  66.3 47.2 %all-to-all-start.3 = ((bf16[16,2,27648]{2,1,0:T(2,128)(2,1)}), bf16[16,2,27648]{2,1,0:T(2,128)(2,1)S(1)}, u32[]{:S(2)}, u32[]{:S(2)}) async-start(bf16[16,2,27648]{2,1,0:T(2,128)(2,1)} %reshape.299), calls=%async_computation.3 | async-start | bytes 3538944 | tf_op jit(solution)/shard_map/all_to_all | solution.py:31
  113.4 105.0 %all-to-all-start.1 = ((bf16[16,2,73728]{2,1,0:T(2,128)(2,1)}), bf16[16,2,73728]{2,1,0:T(2,128)(2,1)}, u32[]{:S(2)}, u32[]{:S(2)}) async-start(bf16[16,2,73728]{2,1,0:T(2,128)(2,1)} %reshape.295), calls=%async_computation.1 | async-start | bytes 9437184 | tf_op jit(solution)/shard_map/all_to_all | solution.py:30
  118.1 197.1 %all-gather.2.cloned.1.call-start = ((), (), s32[]{:S(2)}) async-start(), calls=%async_computation.6 | async-start | bytes 4718592 | tf_op jit(solution)/shard_map/all_gather | solution.py:45
  118.8 364.6 %reduce-scatter.2.cloned.1.call-start = ((), (), s32[]{:S(2)}) async-start(), calls=%async_computation.7 | async-start | bytes 4718592 | tf_op jit(solution)/shard_map/reduce_scatter | solution.py:52
  309.8 5.3 %copy-start.4 = (bf16[1152,768]{0,1:T(8,128)(2,1)S(1)}, bf16[1152,768]{0,1:T(8,128)(2,1)}, u32[]{:S(2)}) copy-start(bf16[1152,768]{0,1:T(8,128)(2,1)} %copy.44) | copy-start | bytes 5308420
  325.6 55.2 %all-to-all-start.4 = ((bf16[16,1,72]{2,1,0:T(2,128)(2,1)}), bf16[16,1,72]{2,1,0:T(2,128)(2,1)S(1)}, u32[]{:S(2)}, u32[]{:S(2)}) async-start(bf16[16,1,72]{2,1,0:T(2,128)(2,1)} %convert_element_type.105), calls=%async_computation.4 | async-start | bytes 16384 | tf_op jit(solution)/shard_map/all_to_all | solution.py:65
  380.8 47.3 %all-to-all-start.2 = ((bf16[16,2,27648]{2,1,0:T(2,128)(2,1)}), bf16[16,2,27648]{2,1,0:T(2,128)(2,1)S(1)}, u32[]{:S(2)}, u32[]{:S(2)}) async-start(bf16[16,2,27648]{2,1,0:T(2,128)(2,1)} %reshape.297), calls=%async_computation.2 | async-start | bytes 3538944 | tf_op jit(solution)/shard_map/all_to_all | solution.py:64
  475.4 8.0 %copy-start.1 = (bf16[128,8,768]{2,1,0:T(8,128)(2,1)S(1)}, bf16[128,8,768]{2,1,0:T(8,128)(2,1)}, u32[]{:S(2)}) copy-start(bf16[128,8,768]{2,1,0:T(8,128)(2,1)} %param.6) | copy-start | bytes 4718596
Sparse Core Ops, SparseCore 0:
  120.5 46.1 all-gather.1
  307.6 47.1 reduce-scatter.1
where the time goes:
time: 500 us; the launch traced here: 490 us
  other arithmetic  203 us (41%)
  local copies, waits for them, and re-layouts  136 us (27%)
  waiting for transfers between devices  86.7 us (17%)
  starting transfers between devices  32.6 us (7%)
  matrix products  17.9 us (4%)
  between operations  14.6 us (3%)
    all_to_all x2, other arithmetic, local(): lax.all_to_all(back_act, ('seq', 'expert'), split_axis=0, concat_axis=0,...  77.5 us
    convert_element_type x1, other arithmetic, local(): (recv_prob[:, None] * recv_grad.astype(jnp.float32)).astype(jnp.bfloat16)  62.7 us
    unnamed x19, local copies, waits for them, and re-layouts  41.1 us
    all_to_all x1, other arithmetic, local(): lax.all_to_all(send_act, ('seq', 'expert'), split_axis=0, concat_axis=0,...  39 us
    all_to_all x1, waiting for transfers between devices, local(): lax.all_to_all(back_act, ('seq', 'expert'), split_axis=0, concat_axis=0,...  33.8 us
    all_to_all x1, waiting for transfers between devices, local(): lax.all_to_all(send_grad, ('seq', 'expert'), split_axis=0, concat_axis=0,...  30.1 us
    mul x2, local copies, waits for them, and re-layouts, local(): recv_prob[:, None] * recv_grad.astype(jnp.float32)  22 us
    all_to_all x1, waiting for transfers between devices, local(): lax.all_to_all(send_act, ('seq', 'expert'), split_axis=0, concat_axis=0,...  22 us
  transfers between devices with their start and end apart: 7, of which 3 were waited for; matrix products, arithmetic and copies ran while one was open for 70% of the time, Pallas kernels for 0%

commit v1 on v0

--- a/solution.py
+++ b/solution.py
@@ -2,6 +2,30 @@
 import jax.numpy as jnp
 from jax import lax
 from jax.sharding import PartitionSpec as P
+
+
+def split_up(x, dim, peers):
+    shape = x.shape
+    blocks = x.reshape(*shape[:dim], peers, shape[dim] // peers, *shape[dim + 1 :])
+    return jnp.moveaxis(blocks, dim, 0)
+
+
+def in_order(pieces, dim):
+    pieces = jnp.moveaxis(pieces, 0, dim)
+    shape = pieces.shape
+    return pieces.reshape(*shape[:dim], shape[dim] * shape[dim + 1], *shape[dim + 2 :])
+
+
+def exchange_directly(x, axis, split_dim, concat_dim):
+    length, index = (lax.axis_size(axis), lax.axis_index(axis))
+    tiles = split_up(x, split_dim, length)
+    whole = tiles
+    for step in range(1, length):
+        target, source = ((index + step) % length, (index - step) % length)
+        sent = lax.dynamic_index_in_dim(tiles, target, 0)
+        other = lax.ppermute(sent, axis, [(i, (i + step) % length) for i in range(length)])
+        whole = lax.dynamic_update_slice_in_dim(whole, other, source, axis=0)
+    return in_order(whole, concat_dim)
 
 
 def local(out_grad, saved_act, gate_probs, routes, w_down):
@@ -28,7 +52,7 @@
     send_prob = prob_rows.reshape(owners, most_rows)
     arrived = (
         lax.all_to_all(send_grad, ("seq", "expert"), split_axis=0, concat_axis=0, tiled=True),
-        lax.all_to_all(send_act, ("seq", "expert"), split_axis=0, concat_axis=0, tiled=True),
+        exchange_directly(send_act, ("seq", "expert"), 0, 0),
         lax.all_to_all(
             send_prob.astype(jnp.bfloat16),
             ("seq", "expert"),

time: 500 us -> 619 us (1.24)
  local copies, waits for them, and re-layouts: 136 us -> 196 us
  waiting for transfers between devices: 86.7 us -> 145 us
  starting transfers between devices: 32.6 us -> 80.3 us
  other arithmetic: 203 us -> 160 us
    ppermute x0 -> x15, waiting for transfers between devices: none -> 112 us  [exchange_directly(): lax.ppermute(sent, axis, [(i, (i + step) % length) for i in range(length)])]
    dynamic_update_slice x0 -> x15, local copies, waits for them, and re-layouts: none -> 69.9 us  [exchange_directly(): whole = lax.dynamic_update_slice_in_dim(whole, other, source, axis=0)]
    all_to_all x1 -> x0, other arithmetic: 39 us -> none  [local(): lax.all_to_all(send_act, ('seq', 'expert'), split_axis=0, concat_axis=0,...]
    ppermute x0 -> x15, starting transfers between devices: none -> 37.3 us  [exchange_directly(): lax.ppermute(sent, axis, [(i, (i + step) % length) for i in range(length)])]
    all_to_all x1, waiting for transfers between devices: 30.1 us -> 0.01 us  [local(): lax.all_to_all(send_grad, ('seq', 'expert'), split_axis=0, concat_axis=0,...]
    all_to_all x1 -> x0, waiting for transfers between devices: 22 us -> none  [local(): lax.all_to_all(send_act, ('seq', 'expert'), split_axis=0, concat_axis=0,...]
    all_to_all x1, starting transfers between devices: 8.08 us -> 22.4 us  [local(): lax.all_to_all(back_prob.astype(jnp.bfloat16), ('seq', 'expert'), split_a...]
    unnamed x19 -> x25, local copies, waits for them, and re-layouts: 41.1 us -> 31.8 us
  transfers between devices with their start and end apart: 7 -> 21, of which waited for: 3 -> 4; matrix products, arithmetic and copies ran while one was open for 70% -> 58% of each run, Pallas kernels for 0% -> 0%
where the time goes in v1:
time: 619 us; the launch traced here: 613 us
  local copies, waits for them, and re-layouts  196 us (32%)
  other arithmetic  160 us (26%)
  waiting for transfers between devices  145 us (23%)
  starting transfers between devices  80.3 us (13%)
  matrix products  15.6 us (3%)
  between operations  15.4 us (2%)
    ppermute x15, waiting for transfers between devices, exchange_directly(): lax.ppermute(sent, axis, [(i, (i + step) % length) for i in range(length)])  112 us
    all_to_all x2, other arithmetic, local(): lax.all_to_all(back_act, ('seq', 'expert'), split_axis=0, concat_axis=0,...  76.3 us
    dynamic_update_slice x15, local copies, waits for them, and re-layouts, exchange_directly(): whole = lax.dynamic_update_slice_in_dim(whole, other, source, axis=0)  69.9 us
    convert_element_type x1, other arithmetic, local(): (recv_prob[:, None] * recv_grad.astype(jnp.float32)).astype(jnp.bfloat16)  62.9 us
    ppermute x15, starting transfers between devices, exchange_directly(): lax.ppermute(sent, axis, [(i, (i + step) % length) for i in range(length)])  37.3 us
    all_to_all x1, waiting for transfers between devices, local(): lax.all_to_all(back_act, ('seq', 'expert'), split_axis=0, concat_axis=0,...  33.3 us
    unnamed x25, local copies, waits for them, and re-layouts  31.8 us
    all_to_all x1, starting transfers between devices, local(): lax.all_to_all(back_prob.astype(jnp.bfloat16), ('seq', 'expert'), split_a...  22.4 us
  transfers between devices with their start and end apart: 21, of which 4 were waited for; matrix products, arithmetic and copies ran while one was open for 58% of the time, Pallas kernels for 0%

profile of v1, /device:TPU:0, one launch (start us, length us, event | category | flops | bytes accessed | tf_op | source)
XLA Modules:
  0.0 612.7 jit_solution(5694775047393730923)
XLA Ops:
  19.3 7.4 %all-to-all-start = ((bf16[16,1,72]{2,1,0:T(2,128)(2,1)}), bf16[16,1,72]{2,1,0:T(2,128)(2,1)S(1)}, u32[]{:S(2)}, u32[]{:S(2)}) async-start(bf16[16,1,72]{2,1,0:T(2,128)(2,1)} %convert_element_type.104), calls=%async_computation | async-start | bytes 16384 | tf_op jit(solution)/shard_map/all_to_all | solution.py:56
  38.3 5.9 gather_fusion
  44.2 5.3 gather.25
  55.0 6.7 %reduce.13 = bf16[16,147456]{1,0:T(8,128)(2,1)} reduce(bf16[16,1,147456]{2,0,1:T(8,128)(2,1)} %broadcast_select_fusion, bf16[]{:T(256)} %broadcast.163), dimensions={1}, to_apply=%copy.39.reduce_sub_computation | reduce | bytes 9437186 | tf_op jit(solution)/shard_map/jit(_take)/select_n | solution.py:48
  61.7 7.3 %reshape.289 = bf16[16,2,73728]{2,1,0:T(2,128)(2,1)} reshape(bf16[16,147456]{1,0:T(8,128)(2,1)} %reduce.13) | data formatting | bytes 9437184
  77.5 6.2 %all-to-all-start.1 = ((bf16[16,2,73728]{2,1,0:T(2,128)(2,1)}), bf16[16,2,73728]{2,1,0:T(2,128)(2,1)}, u32[]{:S(2)}, u32[]{:S(2)}) async-start(bf16[16,2,73728]{2,1,0:T(2,128)(2,1)} %reshape.289), calls=%async_computation.1 | async-start | bytes 9437184 | tf_op jit(solution)/shard_map/all_to_all | solution.py:54
  98.5 71.4 %collective-permute-done = bf16[1,1,55296]{2,0,1:T(2,128)(2,1)S(1)} collective-permute-done((bf16[1,1,55296]{2,0,1:T(2,128)(2,1)S(1)}, bf16[1,1,55296]{2,0,1:T(2,128)(2,1)S(1)}, u32[]{:S(2)}, u32[]{:S(2)}) %collective-permute-start) | collective-permute-done | bytes 110624 | tf_op jit(solution)/shard_map/ppermute | solution.py:26
  175.1 38.0 %collective-permute-done.2 = bf16[1,1,55296]{2,0,1:T(2,128)(2,1)S(1)} collective-permute-done((bf16[1,1,55296]{2,0,1:T(2,128)(2,1)S(1)}, bf16[1,1,55296]{2,0,1:T(2,128)(2,1)S(1)}, u32[]{:S(2)}, u32[]{:S(2)}) %collective-permute-start.2) | collective-permute-done | bytes 110624 | tf_op jit(solution)/shard_map/ppermute | solution.py:26
  213.9 5.2 collective-permute-start.8
  219.1 8.3 %collective-permute-start.9 = (bf16[1,1,55296]{2,0,1:T(2,128)(2,1)S(1)}, bf16[1,1,55296]{2,0,1:T(2,128)(2,1)}, u32[]{:S(2)}, u32[]{:S(2)}) collective-permute-start(bf16[1,1,55296]{2,0,1:T(2,128)(2,1)S(1)} %get-tuple-element.25), channel_id=1, source_target_pairs={{0,10},{1,11},{2,12},{3,13},{4,14},{5,15},{6,0},{7,1},{8,2},{9,3},... | collective-permute-start | bytes 331784 | tf_op jit(solution)/shard_map/ppermute | solution.py:26
  244.0 17.5 %mul.61 = f32[16,1,147456]{2,1,0:T(1,128)} reshape(f32[16,72,2048]{2,1,0:T(8,128)} %mul.60) | data formatting | bytes 18874368 | tf_op jit(solution)/shard_map/mul | solution.py:75
  332.5 12.8 %reshape.290 = bf16[16,1,147456]{2,1,0:T(2,128)(2,1)} reshape(bf16[16,2,73728]{2,1,0:T(2,128)(2,1)} %all-to-all-done.1) | data formatting | bytes 9437184
  345.3 62.9 %convert_reduce_fusion = (bf16[16,147456]{1,0:T(8,128)(2,1)}, bf16[16,147456]{1,0:T(8,128)(2,1)}) fusion(f32[16,1,147456]{2,1,0:T(1,128)} %mul.61, bf16[16,1,147456]{2,1,0:T(2,128)(2,1)} %reshape.290), kind=kLoop, calls=%fused_computation.6 | loop fusion | flops 7077888 | bytes 23592960 | tf_op jit(solution)/shard_map/convert_element_type | solution.py:75
  413.4 8.1 %convolution_convert_fusion = bf16[768,2048]{1,0:T(8,128)(2,1)} fusion(bf16[1152,768]{1,0:T(8,128)(2,1)S(1)} %reshape_reshape.4, bf16[1152,2048]{1,0:T(8,128)(2,1)} %convert_element_type.99), kind=kOutput, calls=%fused_computation.9 | convolution fusion | flops 3625451520 | bytes 9633792 | tf_op jit(solution)/shard_map/dot_general | solution.py:77
  422.6 5.2 reshape.213
  427.9 7.6 %fusion = f32[1152,768]{0,1:T(8,128)S(1)} fusion(bf16[1152,2048]{1,0:T(8,128)(2,1)} %reshape.213, bf16[1,768,2048]{2,1,0:T(8,128)(2,1)} %all-gather.2.cloned.1.call-done), kind=kOutput, calls=%fused_computation.10 | convolution fusion | flops 3623878656 | bytes 11403264 | tf_op jit(solution)/shard_map/dot_general | solution.py:67
  436.8 22.4 %all-to-all-start.3 = ((bf16[16,1,72]{2,1,0:T(2,128)(2,1)}), bf16[16,1,72]{2,1,0:T(2,128)(2,1)S(1)}, u32[]{:S(2)}, u32[]{:S(2)}) async-start(bf16[16,1,72]{2,1,0:T(2,128)(2,1)} %convert_element_type.105), calls=%async_computation.3 | async-start | bytes 16384 | tf_op jit(solution)/shard_map/all_to_all | solution.py:89
  463.8 38.5 %reduce.14 = bf16[16,55296]{1,0:T(8,128)(2,1)S(1)} reduce(bf16[16,1,55296]{2,1,0:T(2,128)(2,1)} %all_to_all.23, bf16[]{:T(256)} %broadcast.163), dimensions={1}, to_apply=%all_to_all.23.reduce_sub_computation | reduce | bytes 3538946 | tf_op jit(solution)/shard_map/all_to_all | solution.py:88
  504.7 6.5 %all-to-all-start.2 = ((bf16[16,2,27648]{2,1,0:T(2,128)(2,1)}), bf16[16,2,27648]{2,1,0:T(2,128)(2,1)S(1)}, u32[]{:S(2)}, u32[]{:S(2)}) async-start(bf16[16,2,27648]{2,1,0:T(2,128)(2,1)} %reshape.291), calls=%async_computation.2 | async-start | bytes 3538944 | tf_op jit(solution)/shard_map/all_to_all | solution.py:88
  511.9 6.1 %gather_fusion.3 = f32[1024]{0:T(1024)S(1)} fusion(f32[1152]{0:T(1024)S(1)} %reshape.218, s32[1024]{0:T(1024)S(1)} %broadcast_clamp_fusion), kind=kCustom, calls=%fused_computation.3 | custom fusion | bytes 12288 | tf_op jit(solution)/shard_map/jit(_take)/gather | solution.py:100
  518.9 33.3 %all-to-all-done.2 = bf16[16,2,27648]{2,1,0:T(2,128)(2,1)S(1)} async-done(((bf16[16,2,27648]{2,1,0:T(2,128)(2,1)}), bf16[16,2,27648]{2,1,0:T(2,128)(2,1)S(1)}, u32[]{:S(2)}, u32[]{:S(2)}) %all-to-all-start.2) | async-done | bytes 1769504 | tf_op jit(solution)/shard_map/all_to_all | solution.py:88
  552.2 6.3 %reshape.292 = bf16[16,1,55296]{2,1,0:T(2,128)(2,1)} reshape(bf16[16,2,27648]{2,1,0:T(2,128)(2,1)S(1)} %all-to-all-done.2) | data formatting | bytes 3538944
  558.5 37.8 %reduce.2 = bf16[16,55296]{1,0:T(8,128)(2,1)S(1)} reduce(bf16[16,1,55296]{2,1,0:T(2,128)(2,1)} %reshape.292, bf16[]{:T(256)} %constant.310), dimensions={1}, to_apply=%all_to_all.21.reduce_sub_computation | reduce | bytes 3538946 | tf_op jit(solution)/shard_map/all_to_all | solution.py:88
  597.2 5.6 gather_fusion.1
  (127 shorter events, 164.9 us)
Async XLA Ops:
  7.2 64.0 %copy-start = (bf16[128,8,768]{2,1,0:T(8,128)(2,1)S(1)}, bf16[128,8,768]{2,1,0:T(8,128)(2,1)}, u32[]{:S(2)}) copy-start(bf16[128,8,768]{2,1,0:T(8,128)(2,1)} %param.6) | copy-start | bytes 4718596
  8.1 25.4 %copy-start.4 = (s32[128,8]{1,0:T(8,128)}, s32[128,8]{1,0:T(8,128)S(1)}, u32[]{:S(2)}) copy-start(s32[128,8]{1,0:T(8,128)S(1)} %copy.32) | copy-start | bytes 12292
  14.3 17.1 %copy-start.7 = (s32[1024,1]{0,1:T(1,128)}, s32[1024,1]{0,1:T(1,128)S(1)}, u32[]{:S(2)}) copy-start(s32[1024,1]{0,1:T(1,128)S(1)} %compare_select_fusion.1) | copy-start | bytes 12292
  19.3 58.2 %all-to-all-start = ((bf16[16,1,72]{2,1,0:T(2,128)(2,1)}), bf16[16,1,72]{2,1,0:T(2,128)(2,1)S(1)}, u32[]{:S(2)}, u32[]{:S(2)}) async-start(bf16[16,1,72]{2,1,0:T(2,128)(2,1)} %convert_element_type.104), calls=%async_computation | async-start | bytes 16384 | tf_op jit(solution)/shard_map/all_to_all | solution.py:56
  77.5 254.9 %all-to-all-start.1 = ((bf16[16,2,73728]{2,1,0:T(2,128)(2,1)}), bf16[16,2,73728]{2,1,0:T(2,128)(2,1)}, u32[]{:S(2)}, u32[]{:S(2)}) async-start(bf16[16,2,73728]{2,1,0:T(2,128)(2,1)} %reshape.289), calls=%async_computation.1 | async-start | bytes 9437184 | tf_op jit(solution)/shard_map/all_to_all | solution.py:54
  83.7 344.2 %all-gather.2.cloned.1.call-start = ((), (), s32[]{:S(2)}) async-start(), calls=%async_computation.5 | async-start | bytes 4718592 | tf_op jit(solution)/shard_map/all_gather | solution.py:69
  90.0 79.9 %collective-permute-start = (bf16[1,1,55296]{2,0,1:T(2,128)(2,1)S(1)}, bf16[1,1,55296]{2,0,1:T(2,128)(2,1)S(1)}, u32[]{:S(2)}, u32[]{:S(2)}) collective-permute-start(bf16[1,1,55296]{2,0,1:T(2,128)(2,1)S(1)} %get-tuple-element.34), channel_id=1, source_target_pairs={{0,1},{1,2},{2,3},{3,4},{4,5},{5,6},{6,7},{7,8},{8,9},{9,10},{10,1... | collective-permute-start | bytes 331784 | tf_op jit(solution)/shard_map/ppermute | solution.py:26
  91.9 78.0 %collective-permute-start.1 = (bf16[1,1,55296]{2,0,1:T(2,128)(2,1)S(1)}, bf16[1,1,55296]{2,0,1:T(2,128)(2,1)S(1)}, u32[]{:S(2)}, u32[]{:S(2)}) collective-permute-start(bf16[1,1,55296]{2,0,1:T(2,128)(2,1)S(1)} %get-tuple-element.33), channel_id=1, source_target_pairs={{0,2},{1,3},{2,4},{3,5},{4,6},{5,7},{6,8},{7,9},{8,10},{9,11},{10,... | collective-permute-start | bytes 331784 | tf_op jit(solution)/shard_map/ppermute | solution.py:26
  93.4 119.7 %collective-permute-start.2 = (bf16[1,1,55296]{2,0,1:T(2,128)(2,1)S(1)}, bf16[1,1,55296]{2,0,1:T(2,128)(2,1)S(1)}, u32[]{:S(2)}, u32[]{:S(2)}) collective-permute-start(bf16[1,1,55296]{2,0,1:T(2,128)(2,1)S(1)} %get-tuple-element.32), channel_id=1, source_target_pairs={{0,3},{1,4},{2,5},{3,6},{4,7},{5,8},{6,9},{7,10},{8,11},{9,12},{10... | collective-permute-start | bytes 331784 | tf_op jit(solution)/shard_map/ppermute | solution.py:26
  95.7 118.1 %collective-permute-start.3 = (bf16[1,1,55296]{2,0,1:T(2,128)(2,1)S(1)}, bf16[1,1,55296]{2,0,1:T(2,128)(2,1)S(1)}, u32[]{:S(2)}, u32[]{:S(2)}) collective-permute-start(bf16[1,1,55296]{2,0,1:T(2,128)(2,1)S(1)} %get-tuple-element.31), channel_id=1, source_target_pairs={{0,4},{1,5},{2,6},{3,7},{4,8},{5,9},{6,10},{7,11},{8,12},{9,13},{1... | collective-permute-start | bytes 331784 | tf_op jit(solution)/shard_map/ppermute | solution.py:26
  96.7 122.4 %collective-permute-start.4 = (bf16[1,1,55296]{2,0,1:T(2,128)(2,1)S(1)}, bf16[1,1,55296]{2,0,1:T(2,128)(2,1)S(1)}, u32[]{:S(2)}, u32[]{:S(2)}) collective-permute-start(bf16[1,1,55296]{2,0,1:T(2,128)(2,1)S(1)} %get-tuple-element.30), channel_id=1, source_target_pairs={{0,5},{1,6},{2,7},{3,8},{4,9},{5,10},{6,11},{7,12},{8,13},{9,14},{... | collective-permute-start | bytes 331784 | tf_op jit(solution)/shard_map/ppermute | solution.py:26
  169.9 57.5 %collective-permute-start.5 = (bf16[1,1,55296]{2,0,1:T(2,128)(2,1)S(1)}, bf16[1,1,55296]{2,0,1:T(2,128)(2,1)S(1)}, u32[]{:S(2)}, u32[]{:S(2)}) collective-permute-start(bf16[1,1,55296]{2,0,1:T(2,128)(2,1)S(1)} %get-tuple-element.29), channel_id=1, source_target_pairs={{0,6},{1,7},{2,8},{3,9},{4,10},{5,11},{6,12},{7,13},{8,14},{9,15},... | collective-permute-start | bytes 331784 | tf_op jit(solution)/shard_map/ppermute | solution.py:26
  169.9 57.9 %collective-permute-start.6 = (bf16[1,1,55296]{2,0,1:T(2,128)(2,1)S(1)}, bf16[1,1,55296]{2,0,1:T(2,128)(2,1)S(1)}, u32[]{:S(2)}, u32[]{:S(2)}) collective-permute-start(bf16[1,1,55296]{2,0,1:T(2,128)(2,1)S(1)} %get-tuple-element.28), channel_id=1, source_target_pairs={{0,7},{1,8},{2,9},{3,10},{4,11},{5,12},{6,13},{7,14},{8,15},{9,0},... | collective-permute-start | bytes 331784 | tf_op jit(solution)/shard_map/ppermute | solution.py:26
  213.1 17.4 %collective-permute-start.7 = (bf16[1,1,55296]{2,0,1:T(2,128)(2,1)S(1)}, bf16[1,1,55296]{2,0,1:T(2,128)(2,1)S(1)}, u32[]{:S(2)}, u32[]{:S(2)}) collective-permute-start(bf16[1,1,55296]{2,0,1:T(2,128)(2,1)S(1)} %get-tuple-element.27), channel_id=1, source_target_pairs={{0,8},{1,9},{2,10},{3,11},{4,12},{5,13},{6,14},{7,15},{8,0},{9,1},... | collective-permute-start | bytes 331784 | tf_op jit(solution)/shard_map/ppermute | solution.py:26
  213.9 22.7 %collective-permute-start.8 = (bf16[1,1,55296]{2,0,1:T(2,128)(2,1)S(1)}, bf16[1,1,55296]{2,0,1:T(2,128)(2,1)}, u32[]{:S(2)}, u32[]{:S(2)}) collective-permute-start(bf16[1,1,55296]{2,0,1:T(2,128)(2,1)S(1)} %get-tuple-element.26), channel_id=1, source_target_pairs={{0,9},{1,10},{2,11},{3,12},{4,13},{5,14},{6,15},{7,0},{8,1},{9,2},... | collective-permute-start | bytes 331784 | tf_op jit(solution)/shard_map/ppermute | solution.py:26
  219.1 17.5 %collective-permute-start.9 = (bf16[1,1,55296]{2,0,1:T(2,128)(2,1)S(1)}, bf16[1,1,55296]{2,0,1:T(2,128)(2,1)}, u32[]{:S(2)}, u32[]{:S(2)}) collective-permute-start(bf16[1,1,55296]{2,0,1:T(2,128)(2,1)S(1)} %get-tuple-element.25), channel_id=1, source_target_pairs={{0,10},{1,11},{2,12},{3,13},{4,14},{5,15},{6,0},{7,1},{8,2},{9,3},... | collective-permute-start | bytes 331784 | tf_op jit(solution)/shard_map/ppermute | solution.py:26
  227.4 78.5 %collective-permute-start.10 = (bf16[1,1,55296]{2,0,1:T(2,128)(2,1)}, bf16[1,1,55296]{2,0,1:T(2,128)(2,1)}, u32[]{:S(2)}, u32[]{:S(2)}) collective-permute-start(bf16[1,1,55296]{2,0,1:T(2,128)(2,1)} %get-tuple-element.24), channel_id=1, source_target_pairs={{0,11},{1,12},{2,13},{3,14},{4,15},{5,0},{6,1},{7,2},{8,3},{9,4},{... | collective-permute-start | bytes 331784 | tf_op jit(solution)/shard_map/ppermute | solution.py:26
  227.8 83.2 %collective-permute-start.11 = (bf16[1,1,55296]{2,0,1:T(2,128)(2,1)}, bf16[1,1,55296]{2,0,1:T(2,128)(2,1)}, u32[]{:S(2)}, u32[]{:S(2)}) collective-permute-start(bf16[1,1,55296]{2,0,1:T(2,128)(2,1)} %get-tuple-element.23), channel_id=1, source_target_pairs={{0,12},{1,13},{2,14},{3,15},{4,0},{5,1},{6,2},{7,3},{8,4},{9,5},{1... | collective-permute-start | bytes 331784 | tf_op jit(solution)/shard_map/ppermute | solution.py:26
  230.5 85.7 %collective-permute-start.12 = (bf16[1,1,55296]{2,0,1:T(2,128)(2,1)}, bf16[1,1,55296]{2,0,1:T(2,128)(2,1)}, u32[]{:S(2)}, u32[]{:S(2)}) collective-permute-start(bf16[1,1,55296]{2,0,1:T(2,128)(2,1)} %get-tuple-element.22), channel_id=1, source_target_pairs={{0,13},{1,14},{2,15},{3,0},{4,1},{5,2},{6,3},{7,4},{8,5},{9,6},{10... | collective-permute-start | bytes 331784 | tf_op jit(solution)/shard_map/ppermute | solution.py:26
  236.6 84.7 %collective-permute-start.13 = (bf16[1,1,55296]{2,0,1:T(2,128)(2,1)}, bf16[1,1,55296]{2,0,1:T(2,128)(2,1)}, u32[]{:S(2)}, u32[]{:S(2)}) collective-permute-start(bf16[1,1,55296]{2,0,1:T(2,128)(2,1)} %get-tuple-element.21), channel_id=1, source_target_pairs={{0,14},{1,15},{2,0},{3,1},{4,2},{5,3},{6,4},{7,5},{8,6},{9,7},{10,... | collective-permute-start | bytes 331784 | tf_op jit(solution)/shard_map/ppermute | solution.py:26
  236.6 89.8 %collective-permute-start.14 = (bf16[1,1,55296]{2,0,1:T(2,128)(2,1)}, bf16[1,1,55296]{2,0,1:T(2,128)(2,1)}, u32[]{:S(2)}, u32[]{:S(2)}) collective-permute-start(bf16[1,1,55296]{2,0,1:T(2,128)(2,1)} %get-tuple-element.20), channel_id=1, source_target_pairs={{0,15},{1,0},{2,1},{3,2},{4,3},{5,4},{6,5},{7,6},{8,7},{9,8},{10,9... | collective-permute-start | bytes 331784 | tf_op jit(solution)/shard_map/ppermute | solution.py:26
  239.3 366.3 %reduce-scatter.2.cloned.1.call-start = ((), (), s32[]{:S(2)}) async-start(), calls=%async_computation.6 | async-start | bytes 4718592 | tf_op jit(solution)/shard_map/reduce_scatter | solution.py:76
  436.8 67.9 %all-to-all-start.3 = ((bf16[16,1,72]{2,1,0:T(2,128)(2,1)}), bf16[16,1,72]{2,1,0:T(2,128)(2,1)S(1)}, u32[]{:S(2)}, u32[]{:S(2)}) async-start(bf16[16,1,72]{2,1,0:T(2,128)(2,1)} %convert_element_type.105), calls=%async_computation.3 | async-start | bytes 16384 | tf_op jit(solution)/shard_map/all_to_all | solution.py:89
  504.7 47.4 %all-to-all-start.2 = ((bf16[16,2,27648]{2,1,0:T(2,128)(2,1)}), bf16[16,2,27648]{2,1,0:T(2,128)(2,1)S(1)}, u32[]{:S(2)}, u32[]{:S(2)}) async-start(bf16[16,2,27648]{2,1,0:T(2,128)(2,1)} %reshape.291), calls=%async_computation.2 | async-start | bytes 3538944 | tf_op jit(solution)/shard_map/all_to_all | solution.py:88
  (6 other events, 33.3 us)
Sparse Core Ops, SparseCore 0:
  239.4 61.8 all-gather.1
  421.6 60.4 reduce-scatter.1
